TPU v7x, 256 devices: a whole 4x4x8 slice. The times are simulated.
256 devices in a mesh: grp: 16 (over z, y_hi), ep: 16 (over y_lo, x, core).
Axes of the slice: x: 4, y: 4 (y_hi: 2, y_lo: 2; y = y_hi * 2 + y_lo), z: 8, core: 2. Of those that a mesh axis runs over, the one named last changes fastest.
Arguments:
- tokens: bfloat16 [49152, 4096], P(('grp', 'ep')), may hold values from -6 to 6
- expert_ids: int32 [49152, 8], P(('grp', 'ep')), may hold values from 0 to 127, all different within a row; in each aligned block of 192 rows (0 to 191, 192 to 383, ...) at most 24 rows name the same one
- gate_probs: float32 [49152, 8], P(('grp', 'ep')), may hold values from 0.02 to 0.25
- placement: int32 [16, 4], P('grp'), may hold values from 0 to 1
- gate_weight: bfloat16 [16, 4096, 3072], P('grp', None, 'ep'), may hold values from -0.09375 to 0.09375
- up_weight: bfloat16 [16, 4096, 3072], P('grp', None, 'ep'), may hold values from -0.09375 to 0.09375
- down_weight: bfloat16 [16, 3072, 4096], P('grp', 'ep'), may hold values from -0.21875 to 0.21875
- out_grad: bfloat16 [49152, 4096], P(('grp', 'ep')), may hold values from -6 to 6
- moment_first: float32 [2, 3072, 4096], P(None, 'ep', 'grp'), may hold values from -2 to 2
- moment_second: float32 [2, 3072, 4096], P(None, 'ep', 'grp'), may hold values from 0.01 to 1
Outputs:
- token_grad: bfloat16 [49152, 4096], P(('grp', 'ep'))
- step_dir: bfloat16 [16, 3072, 4096], P('grp', 'ep')
- new_first: float32 [2, 3072, 4096], P(None, 'ep', 'grp')
- new_second: float32 [2, 3072, 4096], P(None, 'ep', 'grp')
Inputs may be any that keep to these rules, and one draw needn't show every extreme that they name: `expert_ids`: each row names 8 different experts. In the rows of one device no expert is named more than 24 times, a bound that some block reaches. Group g holds expert placement[g, s] * 4 + s in its slot s.
All inputs are finite; a program needn't handle non-finite values.
Results may differ from a plain program's by a relative error of at most 0.015.
Values may be sent and summed in bfloat16 or wider, within the bound.
A program may use at most 128 MiB of HBM per device.

v0:
```python
import math
import jax
import jax.numpy as jnp
from jax import lax
from jax.sharding import PartitionSpec as P

QUARTERS = 4
CANDS = 2
CAP = 24
beta_one = 0.9
beta_two = 0.999
adam_eps = 1e-08
first_fix = 1.0 - math.exp(1000.0 * math.log(0.9))
second_fix = 1.0 - math.exp(1000.0 * math.log(0.999))


def moments(gradient, first_moment, second):
    new_first = beta_one * first_moment + (1.0 - beta_one) * gradient
    new_second = beta_two * second + (1.0 - beta_two) * gradient * gradient
    return (new_first, new_second)


def direction(new_first, new_second):
    return new_first / first_fix / (jnp.sqrt(new_second / second_fix) + adam_eps)


def body(
    tokens,
    expert_ids,
    gate_probs,
    placement,
    gate_weight,
    up_weight,
    down_weight,
    out_grad,
    moment_first,
    moment_second,
):
    num_ep = lax.axis_size("ep")
    slot_count = num_ep // QUARTERS
    tok_count = tokens.shape[0]
    width = tokens.shape[1]
    held_ids = placement[0] * slot_count + jnp.arange(slot_count, dtype=jnp.int32)
    matches = expert_ids[:, :, None] == held_ids[None, None, :]
    hit_rows = jnp.any(matches, axis=1)
    coeffs = jnp.sum(jnp.where(matches, gate_probs[:, :, None], jnp.float32(0.0)), axis=1)
    ranking = jnp.cumsum(hit_rows.astype(jnp.int32), axis=0) - 1
    select_mask = hit_rows.T[:, None, :] & (
        ranking.T[:, None, :] == jnp.arange(CAP, dtype=jnp.int32)[None, :, None]
    )
    select_flat = select_mask.reshape(slot_count * CAP, tok_count).astype(jnp.bfloat16)
    send_tokens = jnp.dot(select_flat, tokens, preferred_element_type=jnp.float32).astype(
        jnp.bfloat16
    )
    send_grads = jnp.dot(select_flat, out_grad, preferred_element_type=jnp.float32).astype(
        jnp.bfloat16
    )
    send_coeffs = jnp.sum(select_mask.astype(jnp.float32) * coeffs.T[:, None, :], axis=2)

    def spread(source):
        shaped = source.reshape(slot_count, 1, CAP, width)
        return jnp.broadcast_to(shaped, (slot_count, QUARTERS, CAP, width)).reshape(
            num_ep, CAP, width
        )

    coeff_spread = jnp.broadcast_to(send_coeffs[:, None, :], (slot_count, QUARTERS, CAP)).reshape(
        num_ep, CAP
    )
    w_gate = gate_weight[0]
    w_up = up_weight[0]
    w_down = down_weight[0]
    recv_tokens, recv_grads, recv_coeffs = (
        lax.all_to_all(spread(send_tokens), "ep", split_axis=0, concat_axis=0, tiled=True),
        lax.all_to_all(spread(send_grads), "ep", split_axis=0, concat_axis=0, tiled=True),
        lax.all_to_all(
            coeff_spread.astype(jnp.bfloat16), "ep", split_axis=0, concat_axis=0, tiled=True
        ).astype(coeff_spread.dtype),
    )
    in_rows = recv_tokens.reshape(num_ep * CAP, width)
    pre_gate = jnp.dot(in_rows, w_gate, preferred_element_type=jnp.float32)
    pre_up = jnp.dot(in_rows, w_up, preferred_element_type=jnp.float32)
    sigmoid_gate = jax.nn.sigmoid(pre_gate)
    activated = pre_gate * sigmoid_gate
    hidden = (activated * pre_up).astype(jnp.bfloat16)
    pre_gate, pre_up, sigmoid_gate, activated, hidden = (
        pre_gate,
        pre_up,
        sigmoid_gate,
        activated,
        hidden,
    )
    scaled = (
        recv_coeffs.reshape(num_ep * CAP)[:, None]
        * recv_grads.reshape(num_ep * CAP, width).astype(jnp.float32)
    ).astype(jnp.bfloat16)
    d_hidden = jnp.einsum("rd,hd->rh", scaled, w_down, preferred_element_type=jnp.float32)
    weight_grad = jnp.einsum("rh,rd->hd", hidden, scaled, preferred_element_type=jnp.float32)
    d_gate = (d_hidden * pre_up * sigmoid_gate * (1.0 + pre_gate * (1.0 - sigmoid_gate))).astype(
        jnp.bfloat16
    )
    d_up = (d_hidden * activated).astype(jnp.bfloat16)
    partial_value = jnp.einsum("rh,dh->rd", d_gate, w_gate, preferred_element_type=jnp.float32)
    partial_value = (
        partial_value + jnp.einsum("rh,dh->rd", d_up, w_up, preferred_element_type=jnp.float32)
    ).astype(jnp.bfloat16)
    returned = lax.all_to_all(
        partial_value.reshape(num_ep, CAP, width), "ep", split_axis=0, concat_axis=0, tiled=True
    )
    combine = jnp.broadcast_to(
        select_mask.reshape(slot_count, 1, CAP, tok_count), (slot_count, QUARTERS, CAP, tok_count)
    )
    combine = combine.reshape(num_ep * CAP, tok_count).astype(jnp.bfloat16)
    token_grad = jnp.einsum(
        "kt,kd->td",
        combine,
        returned.reshape(num_ep * CAP, width),
        preferred_element_type=jnp.float32,
    ).astype(jnp.bfloat16)
    ep_index = lax.axis_index("ep")
    my_cand = lax.dynamic_index_in_dim(placement[0], ep_index // QUARTERS, 0, keepdims=False)
    cand_mask = (jnp.arange(CANDS, dtype=jnp.int32) == my_cand).astype(jnp.float32)
    cand_grads = cand_mask[:, None, None] * weight_grad[None]
    totals = lax.psum(cand_grads.astype(jnp.bfloat16), "grp").astype(jnp.float32)
    full_first, full_second = (
        lax.all_gather(moment_first.astype(jnp.bfloat16), "grp", axis=2, tiled=True).astype(
            moment_first.dtype
        ),
        lax.all_gather(moment_second.astype(jnp.bfloat16), "grp", axis=2, tiled=True).astype(
            moment_second.dtype
        ),
    )
    share_cols = moment_first.shape[2]
    share_start = lax.axis_index("grp") * share_cols
    new_first, new_second = moments(
        lax.dynamic_slice_in_dim(totals, share_start, share_cols, 2), moment_first, moment_second
    )
    own_grad = lax.dynamic_index_in_dim(totals, my_cand, 0, keepdims=True)
    own_first = lax.dynamic_index_in_dim(full_first, my_cand, 0, keepdims=True)
    own_second = lax.dynamic_index_in_dim(full_second, my_cand, 0, keepdims=True)
    copy_first, copy_second = moments(own_grad, own_first, own_second)
    step_dir = direction(copy_first, copy_second).astype(jnp.bfloat16)
    return (token_grad, step_dir, new_first, new_second)


def solution(mesh):
    return jax.shard_map(
        body,
        mesh=mesh,
        in_specs=(
            P(("grp", "ep"), None),
            P(("grp", "ep"), None),
            P(("grp", "ep"), None),
            P("grp", None),
            P("grp", None, "ep"),
            P("grp", None, "ep"),
            P("grp", "ep", None),
            P(("grp", "ep"), None),
            P(None, "ep", "grp"),
            P(None, "ep", "grp"),
        ),
        out_specs=(
            P(("grp", "ep"), None),
            P("grp", "ep", None),
            P(None, "ep", "grp"),
            P(None, "ep", "grp"),
        ),
        check_vma=False,
    )
```

profile of v0, /device:TPU:2, one launch (start us, length us, event | category | flops | bytes accessed | tf_op | source)
XLA Modules:
  0.0 527.4 jit_solution(9174069582011565920)
XLA Ops:
  11.9 5.9 %all-to-all-start = ((bf16[16,1,24]{2,1,0:T(2,128)(2,1)}), bf16[16,1,24]{2,1,0:T(2,128)(2,1)S(1)}, u32[]{:S(2)}, u32[]{:S(2)}) async-start(bf16[16,1,24]{2,1,0:T(2,128)(2,1)} %copy.29), calls=%async_computation | async-start | bytes 16384 | tf_op jit(solution)/shard_map/all_to_all | solution.py:75
  18.0 1.8 convolution_convert_fusion.1
  19.8 2.6 all-to-all-done
  22.4 2.1 broadcast_in_dim.53
  24.5 5.7 %all-to-all-start.2 = ((bf16[16,24,4096]{2,1,0:T(8,128)(2,1)}), bf16[16,24,4096]{2,1,0:T(8,128)(2,1)}, u32[]{:S(2)}, u32[]{:S(2)}) async-start(bf16[16,24,4096]{2,1,0:T(8,128)(2,1)} %bitcast.62), calls=%async_computation.2 | async-start | bytes 6291456 | tf_op jit(solution)/shard_map/all_to_all | solution.py:73
  31.9 41.2 %all-to-all-done.2 = bf16[16,24,4096]{2,1,0:T(8,128)(2,1)} async-done(((bf16[16,24,4096]{2,1,0:T(8,128)(2,1)}), bf16[16,24,4096]{2,1,0:T(8,128)(2,1)}, u32[]{:S(2)}, u32[]{:S(2)}) %all-to-all-start.2) | async-done | bytes 3145760 | tf_op jit(solution)/shard_map/all_to_all | solution.py:73
  73.1 2.1 broadcast_in_dim.29
  75.2 4.5 all-to-all-start.1
  81.1 3.1 fusion.9
  84.2 3.8 fusion.12
  88.0 34.3 %all-to-all-done.1 = bf16[16,24,4096]{2,1,0:T(8,128)(2,1)} async-done(((bf16[16,24,4096]{2,1,0:T(8,128)(2,1)}), bf16[16,24,4096]{2,1,0:T(8,128)(2,1)}, u32[]{:S(2)}, u32[]{:S(2)}) %all-to-all-start.1) | async-done | bytes 3145760 | tf_op jit(solution)/shard_map/all_to_all | solution.py:74
  122.3 2.9 fusion
  126.3 2.3 multiply_convert_fusion
  128.6 181.3 %all-reduce.3.cloned.1.call-done = bf16[2,192,4096]{2,1,0:T(8,128)(2,1)} async-done(((bf16[2,192,4096]{2,1,0:T(8,128)(2,1)}), bf16[2,192,4096]{2,1,0:T(8,128)(2,1)}) %all-reduce.3.cloned.1.call-update) | async-done | bytes 3145744 | tf_op jit(solution)/shard_map/psum | solution.py:123
  309.9 2.7 convert_element_type.124
  312.7 2.7 copy-done.1
  317.2 3.0 multiply_convert_fusion.1
  322.5 2.7 add_convert_fusion
  325.3 4.6 all-to-all-start.3
  331.8 40.9 %all-to-all-done.3 = bf16[16,24,4096]{2,1,0:T(8,128)(2,1)} async-done(((bf16[16,24,4096]{2,1,0:T(8,128)(2,1)}), bf16[16,24,4096]{2,1,0:T(8,128)(2,1)}, u32[]{:S(2)}, u32[]{:S(2)}) %all-to-all-start.3) | async-done | bytes 3145760 | tf_op jit(solution)/shard_map/all_to_all | solution.py:106
  372.8 4.1 convolution_convert_fusion
  376.8 43.8 %all-gather.3.cloned.1.call-done = bf16[2,192,4096]{2,1,0:T(8,128)(2,1)} async-done(((bf16[2,192,256]{2,1,0:T(8,128)(2,1)}), bf16[2,192,4096]{2,1,0:T(8,128)(2,1)}) %all-gather.3.cloned.1.call-update) | async-done | bytes 3145744 | tf_op jit(solution)/shard_map/all_gather | solution.py:125
  420.7 94.2 %all-gather.5.cloned.1.call-done = bf16[2,192,4096]{2,1,0:T(8,128)(2,1)} async-done(((bf16[2,192,256]{2,1,0:T(8,128)(2,1)}), bf16[2,192,4096]{2,1,0:T(8,128)(2,1)}) %all-gather.5.cloned.1.call-update) | async-done | bytes 3145744 | tf_op jit(solution)/shard_map/all_gather | solution.py:128
  514.8 6.1 %fusion.6 = bf16[1,192,4096]{2,1,0:T(8,128)(2,1)} fusion(f32[2,192,4096]{2,1,0:T(8,128)} %copy-done.1, s32[]{:T(128)S(6)} %select_n.25, bf16[2,192,4096]{2,1,0:T(8,128)(2,1)} %all-gather.5.cloned.1.call-done, bf16[2,192,4096]{2,1,0:T(8,128)(2,1)} %all-gather.3.cloned.1.call-done), kind=kLoop, calls=%fused_computation.14 | loop fusion | flops 10223616 | bytes 7864324 | tf_op jit(solution)/shard_map/convert_element_type | solution.py:141
  (55 shorter events, 13.3 us)
Async XLA Ops:
  7.2 74.0 %copy-start = (bf16[1,4096,192]{1,2,0:T(8,128)(2,1)S(1)}, bf16[1,4096,192]{1,2,0:T(8,128)(2,1)}, u32[]{:S(2)}) copy-start(bf16[1,4096,192]{1,2,0:T(8,128)(2,1)} %param.14) | copy-start | bytes 4718596
  11.9 10.5 %all-to-all-start = ((bf16[16,1,24]{2,1,0:T(2,128)(2,1)}), bf16[16,1,24]{2,1,0:T(2,128)(2,1)S(1)}, u32[]{:S(2)}, u32[]{:S(2)}) async-start(bf16[16,1,24]{2,1,0:T(2,128)(2,1)} %copy.29), calls=%async_computation | async-start | bytes 16384 | tf_op jit(solution)/shard_map/all_to_all | solution.py:75
  24.5 48.6 %all-to-all-start.2 = ((bf16[16,24,4096]{2,1,0:T(8,128)(2,1)}), bf16[16,24,4096]{2,1,0:T(8,128)(2,1)}, u32[]{:S(2)}, u32[]{:S(2)}) async-start(bf16[16,24,4096]{2,1,0:T(8,128)(2,1)} %bitcast.62), calls=%async_computation.2 | async-start | bytes 6291456 | tf_op jit(solution)/shard_map/all_to_all | solution.py:73
  75.1 4.6 copy-start.8
  75.2 47.2 %all-to-all-start.1 = ((bf16[16,24,4096]{2,1,0:T(8,128)(2,1)}), bf16[16,24,4096]{2,1,0:T(8,128)(2,1)}, u32[]{:S(2)}, u32[]{:S(2)}) async-start(bf16[16,24,4096]{2,1,0:T(8,128)(2,1)} %bitcast.60), calls=%async_computation.1 | async-start | bytes 6291456 | tf_op jit(solution)/shard_map/all_to_all | solution.py:74
  79.7 4.5 copy-start.2
  79.7 230.2 %all-reduce.3.cloned.1.call-start = ((), (), s32[]{:S(2)}) async-start(), calls=%async_computation.5 | async-start | bytes 6291456 | tf_op jit(solution)/shard_map/psum | solution.py:123
  122.3 2.9 copy-start.3
  128.5 292.1 %all-gather.3.cloned.1.call-start = ((), (), s32[]{:S(2)}) async-start(), calls=%async_computation.4 | async-start | bytes 3342336 | tf_op jit(solution)/shard_map/all_gather | solution.py:125
  309.9 5.4 %copy-start.5 = (f32[2,192,256]{2,1,0:T(8,128)S(1)}, f32[2,192,256]{2,1,0:T(8,128)}, u32[]{:S(2)}) copy-start(f32[2,192,256]{2,1,0:T(8,128)} %param.19) | copy-start | bytes 1179652
  309.9 5.4 %copy-start.6 = (f32[2,192,256]{2,1,0:T(8,128)S(1)}, f32[2,192,256]{2,1,0:T(8,128)}, u32[]{:S(2)}) copy-start(f32[2,192,256]{2,1,0:T(8,128)} %param.18) | copy-start | bytes 1179652
  312.7 2.7 copy-start.1
  316.4 198.4 %all-gather.5.cloned.1.call-start = ((), (), s32[]{:S(2)}) async-start(), calls=%async_computation.6 | async-start | bytes 3342336 | tf_op jit(solution)/shard_map/all_gather | solution.py:128
  317.2 3.0 copy-start.7
  320.2 1.2 copy-start.4
  325.3 47.5 %all-to-all-start.3 = ((bf16[16,24,4096]{2,1,0:T(8,128)(2,1)}), bf16[16,24,4096]{2,1,0:T(8,128)(2,1)}, u32[]{:S(2)}, u32[]{:S(2)}) async-start(bf16[16,24,4096]{2,1,0:T(8,128)(2,1)} %bitcast.61), calls=%async_computation.3 | async-start | bytes 6291456 | tf_op jit(solution)/shard_map/all_to_all | solution.py:106
Sparse Core Ops, SparseCore 0:
  128.7 181.2 all-reduce.2
  316.6 104.0 all-gather.2
  423.1 91.6 all-gather.4
where the time goes:
time: 528 us; the launch traced here: 527 us
  waiting for transfers between devices  439 us (83%)
  other arithmetic  22.7 us (4%)
  starting transfers between devices  20.7 us (4%)
  matrix products  20.5 us (4%)
  between operations  16 us (3%)
  local copies, waits for them, and re-layouts  8.52 us (2%)
    psum x1, waiting for transfers between devices, body(): lax.psum(cand_grads.astype(jnp.bfloat16), 'grp').astype(jnp.float32)  181 us
    all_gather x1, waiting for transfers between devices, body(): lax.all_gather(moment_second.astype(jnp.bfloat16), 'grp', axis=2, tiled=T...  94.2 us
    all_gather x1, waiting for transfers between devices, body(): lax.all_gather(moment_first.astype(jnp.bfloat16), 'grp', axis=2, tiled=True)  43.8 us
    all_to_all x1, waiting for transfers between devices, body(): lax.all_to_all(spread(send_tokens), 'ep', split_axis=0, concat_axis=0, ti...  41.2 us
    all_to_all x1, waiting for transfers between devices, body(): lax.all_to_all(partial_value.reshape(num_ep, CAP, width), 'ep', split_axi...  40.9 us
    all_to_all x1, waiting for transfers between devices, body(): lax.all_to_all(spread(send_grads), 'ep', split_axis=0, concat_axis=0, til...  34.3 us
  transfers between devices with their start and end apart: 7, of which 7 were waited for; matrix products, arithmetic and copies ran while one was open for 5% of the time, Pallas kernels for 0%

commit v1 on v0

--- a/solution.py
+++ b/solution.py
@@ -120,7 +120,9 @@
     my_cand = lax.dynamic_index_in_dim(placement[0], ep_index // QUARTERS, 0, keepdims=False)
     cand_mask = (jnp.arange(CANDS, dtype=jnp.int32) == my_cand).astype(jnp.float32)
     cand_grads = cand_mask[:, None, None] * weight_grad[None]
-    totals = lax.psum(cand_grads.astype(jnp.bfloat16), "grp").astype(jnp.float32)
+    totals = jnp.sum(lax.all_gather(cand_grads.astype(jnp.bfloat16), "grp"), axis=0).astype(
+        jnp.float32
+    )
     full_first, full_second = (
         lax.all_gather(moment_first.astype(jnp.bfloat16), "grp", axis=2, tiled=True).astype(
             moment_first.dtype

time: 528 us -> 968 us (1.83)
  waiting for transfers between devices: 439 us -> 860 us
  other arithmetic: 22.7 us -> 40.9 us
    all_gather x0 -> x1, waiting for transfers between devices: none -> 602 us  [body(): lax.all_gather(cand_grads.astype(jnp.bfloat16), 'grp')]
    psum x1 -> x0, waiting for transfers between devices: 181 us -> none  [body(): lax.psum(cand_grads.astype(jnp.bfloat16), 'grp').astype(jnp.float32)]
    reduce_sum x0 -> x1, other arithmetic: none -> 18.3 us  [body(): jnp.sum(lax.all_gather(cand_grads.astype(jnp.bfloat16), 'grp'), axis=0)]
  transfers between devices with their start and end apart: 7 -> 7, of which waited for: 7 -> 7; matrix products, arithmetic and copies ran while one was open for 5% -> 2% of each run, Pallas kernels for 0% -> 0%
where the time goes in v1:
time: 968 us; the launch traced here: 967 us
  waiting for transfers between devices  860 us (89%)
  other arithmetic  40.9 us (4%)
  starting transfers between devices  21.2 us (2%)
  matrix products  20.5 us (2%)
  between operations  15.9 us (2%)
    all_gather x1, waiting for transfers between devices, body(): lax.all_gather(cand_grads.astype(jnp.bfloat16), 'grp')  602 us
    all_gather x1, waiting for transfers between devices, body(): lax.all_gather(moment_second.astype(jnp.bfloat16), 'grp', axis=2, tiled=T...  94.2 us
    all_gather x1, waiting for transfers between devices, body(): lax.all_gather(moment_first.astype(jnp.bfloat16), 'grp', axis=2, tiled=True)  43.7 us
    all_to_all x1, waiting for transfers between devices, body(): lax.all_to_all(spread(send_tokens), 'ep', split_axis=0, concat_axis=0, ti...  41.2 us
    all_to_all x1, waiting for transfers between devices, body(): lax.all_to_all(partial_value.reshape(num_ep, CAP, width), 'ep', split_axi...  41 us
    all_to_all x1, waiting for transfers between devices, body(): lax.all_to_all(spread(send_grads), 'ep', split_axis=0, concat_axis=0, til...  34.3 us
  transfers between devices with their start and end apart: 7, of which 7 were waited for; matrix products, arithmetic and copies ran while one was open for 2% of the time, Pallas kernels for 0%

profile of v1, /device:TPU:2, one launch (start us, length us, event | category | flops | bytes accessed | tf_op | source)
XLA Modules:
  0.0 966.9 jit_solution(667143558733277540)
XLA Ops:
  11.9 5.9 all-to-all-start
  19.8 2.6 all-to-all-done
  22.4 2.1 broadcast_in_dim.53
  24.5 5.7 all-to-all-start.2
  31.9 41.2 %all-to-all-done.2 = bf16[16,24,4096]{2,1,0:T(8,128)(2,1)} async-done(((bf16[16,24,4096]{2,1,0:T(8,128)(2,1)}), bf16[16,24,4096]{2,1,0:T(8,128)(2,1)}, u32[]{:S(2)}, u32[]{:S(2)}) %all-to-all-start.2) | async-done | bytes 3145760 | tf_op jit(solution)/shard_map/all_to_all | solution.py:73
  73.1 2.1 broadcast_in_dim.29
  75.2 4.5 all-to-all-start.1
  81.2 3.1 fusion.9
  84.2 3.8 fusion.12
  88.0 34.3 %all-to-all-done.1 = bf16[16,24,4096]{2,1,0:T(8,128)(2,1)} async-done(((bf16[16,24,4096]{2,1,0:T(8,128)(2,1)}), bf16[16,24,4096]{2,1,0:T(8,128)(2,1)}, u32[]{:S(2)}, u32[]{:S(2)}) %all-to-all-start.1) | async-done | bytes 3145760 | tf_op jit(solution)/shard_map/all_to_all | solution.py:74
  122.3 2.9 fusion
  126.3 2.2 multiply_convert_fusion
  128.5 602.3 %all-gather.6.cloned.1.call-done = bf16[16,2,192,4096]{3,2,1,0:T(8,128)(2,1)} async-done(((bf16[1,2,192,4096]{3,2,1,0:T(8,128)(2,1)}), bf16[16,2,192,4096]{3,2,1,0:T(8,128)(2,1)}) %all-gather.6.cloned.1.call-update) | async-done | bytes 50331664 | tf_op jit(solution)/shard_map/all_gather | solution.py:123
  730.9 18.3 %reduce_sum.32 = bf16[2,192,4096]{2,1,0:T(8,128)(2,1)} reduce(bf16[16,2,192,4096]{3,2,1,0:T(8,128)(2,1)} %all-gather.6.cloned.1.call-done, bf16[]{:T(256)} %constant.67.clone.1), dimensions={0}, to_apply=%region_5.6 | reduce | flops 23592960 | bytes 53477376 | tf_op jit(solution)/shard_map/reduce_sum | solution.py:123
  749.2 2.7 convert_element_type.133
  751.9 2.7 copy-done.1
  756.4 3.0 multiply_convert_fusion.1
  761.8 2.7 add_convert_fusion
  764.5 4.8 all-to-all-start.3
  771.3 41.0 %all-to-all-done.3 = bf16[16,24,4096]{2,1,0:T(8,128)(2,1)} async-done(((bf16[16,24,4096]{2,1,0:T(8,128)(2,1)}), bf16[16,24,4096]{2,1,0:T(8,128)(2,1)}, u32[]{:S(2)}, u32[]{:S(2)}) %all-to-all-start.3) | async-done | bytes 3145760 | tf_op jit(solution)/shard_map/all_to_all | solution.py:106
  812.4 4.1 convolution_convert_fusion
  816.4 43.7 %all-gather.4.cloned.1.call-done = bf16[2,192,4096]{2,1,0:T(8,128)(2,1)} async-done(((bf16[2,192,256]{2,1,0:T(8,128)(2,1)}), bf16[2,192,4096]{2,1,0:T(8,128)(2,1)}) %all-gather.4.cloned.1.call-update) | async-done | bytes 3145744 | tf_op jit(solution)/shard_map/all_gather | solution.py:127
  860.2 94.2 %all-gather.8.cloned.1.call-done = bf16[2,192,4096]{2,1,0:T(8,128)(2,1)} async-done(((bf16[2,192,256]{2,1,0:T(8,128)(2,1)}), bf16[2,192,4096]{2,1,0:T(8,128)(2,1)}) %all-gather.8.cloned.1.call-update) | async-done | bytes 3145744 | tf_op jit(solution)/shard_map/all_gather | solution.py:130
  954.3 6.1 fusion.6
  (56 shorter events, 15.1 us)
Async XLA Ops:
  7.2 74.0 %copy-start = (bf16[1,4096,192]{1,2,0:T(8,128)(2,1)S(1)}, bf16[1,4096,192]{1,2,0:T(8,128)(2,1)}, u32[]{:S(2)}) copy-start(bf16[1,4096,192]{1,2,0:T(8,128)(2,1)} %param.14) | copy-start | bytes 4718596
  11.9 10.5 %all-to-all-start = ((bf16[16,1,24]{2,1,0:T(2,128)(2,1)}), bf16[16,1,24]{2,1,0:T(2,128)(2,1)S(1)}, u32[]{:S(2)}, u32[]{:S(2)}) async-start(bf16[16,1,24]{2,1,0:T(2,128)(2,1)} %copy.29), calls=%async_computation | async-start | bytes 16384 | tf_op jit(solution)/shard_map/all_to_all | solution.py:75
  24.5 48.6 %all-to-all-start.2 = ((bf16[16,24,4096]{2,1,0:T(8,128)(2,1)}), bf16[16,24,4096]{2,1,0:T(8,128)(2,1)}, u32[]{:S(2)}, u32[]{:S(2)}) async-start(bf16[16,24,4096]{2,1,0:T(8,128)(2,1)} %bitcast.62), calls=%async_computation.2 | async-start | bytes 6291456 | tf_op jit(solution)/shard_map/all_to_all | solution.py:73
  75.1 4.6 copy-start.8
  75.2 47.2 %all-to-all-start.1 = ((bf16[16,24,4096]{2,1,0:T(8,128)(2,1)}), bf16[16,24,4096]{2,1,0:T(8,128)(2,1)}, u32[]{:S(2)}, u32[]{:S(2)}) async-start(bf16[16,24,4096]{2,1,0:T(8,128)(2,1)} %bitcast.60), calls=%async_computation.1 | async-start | bytes 6291456 | tf_op jit(solution)/shard_map/all_to_all | solution.py:74
  79.7 4.5 copy-start.2
  79.7 651.2 %all-gather.6.cloned.1.call-start = ((), (), s32[]{:S(2)}) async-start(), calls=%async_computation.5 | async-start | bytes 53477376 | tf_op jit(solution)/shard_map/all_gather | solution.py:123
  122.3 2.9 copy-start.3
  128.5 731.7 %all-gather.4.cloned.1.call-start = ((), (), s32[]{:S(2)}) async-start(), calls=%async_computation.4 | async-start | bytes 3342336 | tf_op jit(solution)/shard_map/all_gather | solution.py:127
  749.2 5.4 copy-start.5
  749.2 5.4 copy-start.6
  751.9 2.7 copy-start.1
  755.7 198.7 %all-gather.8.cloned.1.call-start = ((), (), s32[]{:S(2)}) async-start(), calls=%async_computation.6 | async-start | bytes 3342336 | tf_op jit(solution)/shard_map/all_gather | solution.py:130
  756.4 3.0 copy-start.7
  759.5 1.2 copy-start.4
  764.5 47.8 %all-to-all-start.3 = ((bf16[16,24,4096]{2,1,0:T(8,128)(2,1)}), bf16[16,24,4096]{2,1,0:T(8,128)(2,1)}, u32[]{:S(2)}, u32[]{:S(2)}) async-start(bf16[16,24,4096]{2,1,0:T(8,128)(2,1)} %bitcast.61), calls=%async_computation.3 | async-start | bytes 6291456 | tf_op jit(solution)/shard_map/all_to_all | solution.py:106
Sparse Core Ops, SparseCore 0:
  128.6 602.2 all-gather.5
  755.8 104.3 all-gather.3
  862.6 91.6 all-gather.7
